TPU v7x, 512 devices: a whole 4x4x16 slice. The times are simulated.
512 devices in a mesh: dom: 64 (over x, z), orb: 8 (over y, core).
Axes of the slice: x: 4, y: 4, z: 16, core: 2. Of those that a mesh axis runs over, the one named last changes fastest.
Arguments:
- orbitals: bfloat16 [3072, 64, 512], P('dom', 'orb'), may hold values from -6 to 6
- adjoint_source: bfloat16 [3072, 64, 512], P('dom', 'orb'), may hold values from -6 to 6
- eigenvalues: float32 [64], P('orb'), may hold values from -1 to -0.25
- cell_scale: float32 [3072], P('dom'), may hold values from 0.4 to 1.6
- base_potential: float32 [3072, 512], P('dom'), may hold values from 0.5 to 1.5
- stiffness: bfloat16 [512, 512], replicated, may hold values from -1.5 to 1.5, as said below
- face_perm: int32 [3072, 64], P('dom'), may hold values from 0 to 63, each once within a row
- restrict: bfloat16 [512, 64], replicated, may hold values from -0.25 to 0.25
- prolong: bfloat16 [64, 512], replicated, may hold values from -0.75 to 0.75
- owner: int32 [3072, 1], P('dom'), may hold values from 0 to 63; in each aligned block of 48 rows (0 to 47, 48 to 95, ...) at most 2 rows name the same one
- pot_slot: int32 [3072], P('dom'), may hold values from 0 to 63
- potential: float32 [4096, 64], P('dom'), may hold values from -6 to 6
Outputs:
- adjoint: bfloat16 [3072, 64, 512], P('dom', 'orb')
- updated: float32 [4096, 64], P('dom')
- applied: bfloat16 [3072, 64, 512], P('dom', 'orb')
Inputs may be any that keep to these rules, and one draw needn't show every extreme that they name: In the rows of one device no owner is named by more than 2 cells. `face_perm`: each row is a permutation. `stiffness`: symmetric.
All inputs are finite; a program needn't handle non-finite values.
Results may differ from a plain program's by a relative error of at most 0.0027.
Values sent between devices are 32-bit elements; how exact they have to be, the bound alone decides.
No kernel may reach another device: no remote copies, remote signals or barrier semaphores. Data moves between devices by JAX's collectives and lax.ppermute only.
A program may use at most 64 MiB of HBM per device.

v0:
```python
import jax
import jax.numpy as jnp
from jax import lax
from jax.sharding import PartitionSpec as P

ITERS = 4
relax = 0.25
step_rate = 0.1


def padded_2(block, sides, width):
    for axis, dim in sides:
        count = lax.axis_size(axis)
        forward = [(i, i + 1) for i in range(count - 1)]
        backward = [(target, source) for source, target in forward]
        low = lax.ppermute(
            lax.slice_in_dim(block, block.shape[dim] - width, None, axis=dim), axis, forward
        )
        high = lax.ppermute(lax.slice_in_dim(block, 0, width, axis=dim), axis, backward)
        block = jnp.concatenate([low, block, high], axis=dim)
    return block


def local(
    orbitals,
    adjoint_source,
    eigenvalues,
    cell_scale,
    base_potential,
    stiffness,
    face_perm,
    restrict,
    prolong,
    owner,
    pot_slot,
    potential,
):
    nodes = stiffness.shape[0]
    faces = face_perm.shape[1]
    pot_rows = potential.shape[0]
    n_domains = lax.axis_size("dom")
    cell_count = owner.shape[0]
    capacity = 2 * ((cell_count + n_domains - 1) // n_domains)
    onehot = (face_perm[:, :, None] == jnp.arange(faces, dtype=jnp.int32)[None, None, :]).astype(
        jnp.float32
    )

    def assemble_local(partial_sum):
        left_face = partial_sum[:, :, :faces]
        right_face = partial_sum[:, :, nodes - faces :]
        sent_right = jnp.einsum("ckj,cok->coj", onehot, right_face, precision=lax.Precision.HIGHEST)
        boundary = jnp.stack([left_face[0], sent_right[-1]], 0)
        padded = padded_2(boundary, (("dom", 0),), 1)
        left_next = jnp.concatenate([left_face[1:], padded[3][None]], 0)
        add_right = jnp.einsum("ckj,coj->cok", onehot, left_next, precision=lax.Precision.HIGHEST)
        add_left = jnp.concatenate([padded[0][None], sent_right[:-1]], 0)
        return jnp.concatenate(
            [
                left_face + add_left,
                partial_sum[:, :, faces : nodes - faces],
                right_face + add_right,
            ],
            2,
        )

    def operator(values_bf, values_full, shift):
        kinetic = jnp.dot(
            values_bf.reshape(-1, nodes), stiffness, preferred_element_type=jnp.float32
        ).reshape(values_full.shape)
        return assemble_local(cell_scale[:, None, None] * kinetic + shift * values_full)

    source = adjoint_source.astype(jnp.float32)
    shift = base_potential[:, None, :] - eigenvalues[None, :, None]
    iterate = relax * source
    for step_index in range(ITERS):
        image = operator(iterate.astype(jnp.bfloat16), iterate, shift)
        iterate = iterate + relax * (source - image)
    adjoint = iterate.astype(jnp.bfloat16)
    partial_density = jnp.sum(orbitals.astype(jnp.float32) * iterate, axis=1)
    restrict_full = restrict.astype(jnp.float32)
    density_term = lax.psum(partial_density, "orb")
    projected = jnp.dot(density_term, restrict_full, precision=lax.Precision.HIGHEST)
    coarse_cols = projected.shape[1]
    dest_owner = owner[:, 0]
    owner_hot = (dest_owner[:, None] == jnp.arange(n_domains, dtype=jnp.int32)[None, :]).astype(
        jnp.int32
    )
    earlier = jnp.cumsum(owner_hot, axis=0) - owner_hot
    rank_within = jnp.sum(earlier * owner_hot, axis=1)
    slot_index = dest_owner * capacity + rank_within
    send_hot_int = (
        slot_index[None, :] == jnp.arange(n_domains * capacity, dtype=jnp.int32)[:, None]
    ).astype(jnp.int32)
    send_hot = send_hot_int.astype(jnp.float32)
    send_values = jnp.dot(send_hot, projected, precision=lax.Precision.HIGHEST).reshape(
        n_domains, capacity, coarse_cols
    )
    send_ids = (jnp.sum(send_hot_int * (pot_slot + 1)[None, :], axis=1) - 1).reshape(
        n_domains, capacity
    )
    recv_values, recv_ids = (
        lax.all_to_all(send_values, "dom", split_axis=0, concat_axis=0, tiled=True),
        lax.all_to_all(send_ids, "dom", split_axis=0, concat_axis=0, tiled=True),
    )
    recv_hot = (
        recv_ids.reshape(-1)[None, :] == jnp.arange(pot_rows, dtype=jnp.int32)[:, None]
    ).astype(jnp.float32)
    summed = jnp.dot(
        recv_hot, recv_values.reshape(-1, coarse_cols), precision=lax.Precision.HIGHEST
    )
    updated = potential - step_rate * summed
    every_pot = lax.all_gather(updated, "dom", axis=0, tiled=True)
    cell_pot = every_pot[dest_owner * pot_rows + pot_slot]
    node_potential = jnp.dot(cell_pot, prolong.astype(jnp.float32), precision=lax.Precision.HIGHEST)
    shift_new = (base_potential + node_potential)[:, None, :]
    applied = operator(orbitals, orbitals.astype(jnp.float32), shift_new).astype(jnp.bfloat16)
    return (adjoint, updated, applied)


def solution(mesh):
    in_specs = (
        P("dom", "orb", None),
        P("dom", "orb", None),
        P("orb"),
        P("dom"),
        P("dom", None),
        P(),
        P("dom", None),
        P(),
        P(),
        P("dom", None),
        P("dom"),
        P("dom", None),
    )
    out_specs = (P("dom", "orb", None), P("dom", None), P("dom", "orb", None))
    return jax.shard_map(local, mesh=mesh, in_specs=in_specs, out_specs=out_specs, check_vma=False)
```

profile of v0, /device:TPU:2, one launch (start us, length us, event | category | flops | bytes accessed | tf_op | source)
XLA Modules:
  0.0 320.8 jit_solution(6365384118985894531)
XLA Ops:
  7.3 1.0 copy-done
  8.2 1.6 fusion.10
  9.8 11.4 %collective-permute-start.1 = (f32[1,8,64]{2,1,0:T(8,128)S(1)}, f32[1,8,64]{2,1,0:T(8,128)S(1)}, u32[]{:S(2)}, u32[]{:S(2)}) collective-permute-start(f32[1,8,64]{2,1,0:T(8,128)S(1)} %slice.159), channel_id=1, source_target_pairs={{8,0},{16,8},{24,16},{32,24},{40,32},{48,40},{56,48},{64,56},{72,6... | collective-permute-start | bytes 6152 | tf_op jit(solution)/shard_map/ppermute | solution.py:19
  21.2 1.4 fusion.9
  22.7 1.9 collective-permute-start
  25.4 1.4 fusion.15
  26.8 3.5 %collective-permute-done = f32[1,8,64]{2,1,0:T(8,128)S(1)} collective-permute-done((f32[1,8,64]{2,1,0:T(8,128)S(1)}, f32[1,8,64]{2,1,0:T(8,128)S(1)}, u32[]{:S(2)}, u32[]{:S(2)}) %collective-permute-start) | collective-permute-done | bytes 2080 | tf_op jit(solution)/shard_map/ppermute | solution.py:16
  30.3 0.8 fusion.11
  31.2 2.6 collective-permute-start.3
  33.8 1.4 fusion.7
  35.5 3.3 %collective-permute-start.2 = (f32[1,8,64]{2,1,0:T(8,128)S(1)}, f32[1,8,64]{2,1,0:T(8,128)S(1)}, u32[]{:S(2)}, u32[]{:S(2)}) collective-permute-start(f32[1,8,64]{2,1,0:T(8,128)S(1)} %slice.162), channel_id=1, source_target_pairs={{0,8},{8,16},{16,24},{24,32},{32,40},{40,48},{48,56},{56,64},{64,7... | collective-permute-start | bytes 6152 | tf_op jit(solution)/shard_map/ppermute | solution.py:16
  38.8 1.4 fusion.16
  40.2 2.9 collective-permute-done.2
  43.2 0.6 fusion.27
  43.8 0.4 fusion.12
  44.2 1.9 collective-permute-start.5
  46.1 1.4 fusion.5
  47.8 3.9 %collective-permute-start.4 = (f32[1,8,64]{2,1,0:T(8,128)S(1)}, f32[1,8,64]{2,1,0:T(8,128)S(1)}, u32[]{:S(2)}, u32[]{:S(2)}) collective-permute-start(f32[1,8,64]{2,1,0:T(8,128)S(1)} %slice.169), channel_id=1, source_target_pairs={{0,8},{8,16},{16,24},{24,32},{32,40},{40,48},{48,56},{56,64},{64,7... | collective-permute-start | bytes 6152 | tf_op jit(solution)/shard_map/ppermute | solution.py:16
  51.8 1.4 fusion.17
  53.2 2.3 collective-permute-done.4
  55.5 0.8 fusion.13
  56.3 1.9 collective-permute-start.7
  58.3 1.4 fusion.3
  60.0 3.9 %collective-permute-start.6 = (f32[1,8,64]{2,1,0:T(8,128)S(1)}, f32[1,8,64]{2,1,0:T(8,128)S(1)}, u32[]{:S(2)}, u32[]{:S(2)}) collective-permute-start(f32[1,8,64]{2,1,0:T(8,128)S(1)} %slice.176), channel_id=1, source_target_pairs={{0,8},{8,16},{16,24},{24,32},{32,40},{40,48},{48,56},{56,64},{64,7... | collective-permute-start | bytes 6152 | tf_op jit(solution)/shard_map/ppermute | solution.py:16
  63.9 1.4 fusion.18
  65.3 2.3 collective-permute-done.6
  67.7 2.1 fusion.24
  69.8 0.8 sub.46
  70.5 5.7 %all-to-all-start = ((s32[64,1,2]{2,1,0:T(1,128)}), s32[64,1,2]{2,1,0:T(1,128)S(1)}, u32[]{:S(2)}, u32[]{:S(2)}) async-start(s32[64,1,2]{2,1,0:T(1,128)} %bitcast.2), calls=%async_computation | async-start | bytes 65536 | tf_op jit(solution)/shard_map/all_to_all | solution.py:103
  76.3 58.1 %all-reduce.2.cloned.1.call-done = f32[48,512]{1,0:T(8,128)} async-done(((f32[48,512]{1,0:T(8,128)}), f32[48,512]{1,0:T(8,128)}) %all-reduce.2.cloned.1.call-update) | async-done | bytes 98320 | tf_op jit(solution)/shard_map/psum | solution.py:81
  134.3 1.1 fusion.90
  135.8 0.7 reshape.85
  136.5 15.9 %all-to-all-start.1 = ((f32[64,1,128]{2,1,0:T(1,128)}), f32[64,1,128]{2,1,0:T(1,128)S(1)}, u32[]{:S(2)}, u32[]{:S(2)}) async-start(f32[64,1,128]{2,1,0:T(1,128)} %reshape.85), calls=%async_computation.1 | async-start | bytes 65536 | tf_op jit(solution)/shard_map/all_to_all | solution.py:102
  152.5 0.5 broadcast.70
  153.0 0.7 reduce.3
  153.8 12.0 %all-to-all-done.1 = f32[64,1,128]{2,1,0:T(1,128)S(1)} async-done(((f32[64,1,128]{2,1,0:T(1,128)}), f32[64,1,128]{2,1,0:T(1,128)S(1)}, u32[]{:S(2)}, u32[]{:S(2)}) %all-to-all-start.1) | async-done | bytes 32800 | tf_op jit(solution)/shard_map/all_to_all | solution.py:102
  165.9 0.5 broadcast.72
  166.4 0.7 reduce.4
  167.2 0.8 fusion.21
  168.0 128.1 %all-gather.2.cloned.1.call-done = f32[4096,64]{1,0:T(8,128)} async-done(((f32[64,64]{1,0:T(8,128)}), f32[4096,64]{1,0:T(8,128)}) %all-gather.2.cloned.1.call-update) | async-done | bytes 1048592 | tf_op jit(solution)/shard_map/all_gather | solution.py:112
  296.1 2.2 gather_fusion
  298.5 0.4 fusion.14
  298.9 4.8 %collective-permute-start.9 = (f32[1,8,64]{2,1,0:T(8,128)S(1)}, f32[1,8,64]{2,1,0:T(8,128)S(1)}, u32[]{:S(2)}, u32[]{:S(2)}) collective-permute-start(f32[1,8,64]{2,1,0:T(8,128)S(1)} %slice.187), channel_id=1, source_target_pairs={{8,0},{16,8},{24,16},{32,24},{40,32},{48,40},{56,48},{64,56},{72,6... | collective-permute-start | bytes 6152 | tf_op jit(solution)/shard_map/ppermute | solution.py:19
  303.7 1.4 fusion.1
  305.4 1.9 collective-permute-start.8
  307.3 1.6 fusion.20
  308.9 4.1 %collective-permute-done.8 = f32[1,8,64]{2,1,0:T(8,128)S(1)} collective-permute-done((f32[1,8,64]{2,1,0:T(8,128)S(1)}, f32[1,8,64]{2,1,0:T(8,128)S(1)}, u32[]{:S(2)}, u32[]{:S(2)}) %collective-permute-start.8) | collective-permute-done | bytes 2080 | tf_op jit(solution)/shard_map/ppermute | solution.py:16
  313.0 1.0 pad_maximum_fusion
  (74 shorter events, 2.8 us)
Async XLA Ops:
  7.2 1.0 copy-start
  7.2 14.0 %copy-start.11 = (s32[48,64]{1,0:T(8,128)S(1)}, s32[48,64]{1,0:T(8,128)}, u32[]{:S(2)}) copy-start(s32[48,64]{1,0:T(8,128)} %param.18) | copy-start | bytes 36868
  7.2 17.4 %copy-start.7 = (s32[48,1]{0,1:T(1,128)S(1)}, s32[48,1]{0,1:T(1,128)}, u32[]{:S(2)}) copy-start(s32[48,1]{0,1:T(1,128)} %param.21) | copy-start | bytes 580
  7.2 17.7 %copy-start.9 = (s32[48]{0:T(128)S(1)}, s32[48]{0:T(128)}, u32[]{:S(2)}) copy-start(s32[48]{0:T(128)} %param.22) | copy-start | bytes 580
  7.2 127.1 %all-reduce.2.cloned.1.call-start = ((), (), s32[]{:S(2)}) async-start(), calls=%async_computation.2 | async-start | bytes 196608 | tf_op jit(solution)/shard_map/psum | solution.py:81
  9.8 15.5 %collective-permute-start.1 = (f32[1,8,64]{2,1,0:T(8,128)S(1)}, f32[1,8,64]{2,1,0:T(8,128)S(1)}, u32[]{:S(2)}, u32[]{:S(2)}) collective-permute-start(f32[1,8,64]{2,1,0:T(8,128)S(1)} %slice.159), channel_id=1, source_target_pairs={{8,0},{16,8},{24,16},{32,24},{40,32},{48,40},{56,48},{64,56},{72,6... | collective-permute-start | bytes 6152 | tf_op jit(solution)/shard_map/ppermute | solution.py:19
  22.7 7.6 %collective-permute-start = (f32[1,8,64]{2,1,0:T(8,128)S(1)}, f32[1,8,64]{2,1,0:T(8,128)S(1)}, u32[]{:S(2)}, u32[]{:S(2)}) collective-permute-start(f32[1,8,64]{2,1,0:T(8,128)S(1)} %slice.155), channel_id=1, source_target_pairs={{0,8},{8,16},{16,24},{24,32},{32,40},{40,48},{48,56},{56,64},{64,7... | collective-permute-start | bytes 6152 | tf_op jit(solution)/shard_map/ppermute | solution.py:16
  25.0 5.3 %copy-start.1 = (bf16[48,8,512]{2,1,0:T(8,128)(2,1)S(1)}, bf16[48,8,512]{2,1,0:T(8,128)(2,1)}, u32[]{:S(2)}) copy-start(bf16[48,8,512]{2,1,0:T(8,128)(2,1)} %param.13) | copy-start | bytes 1179652
  25.1 5.3 %copy-start.3 = (f32[48,512]{1,0:T(8,128)S(1)}, f32[48,512]{1,0:T(8,128)}, u32[]{:S(2)}) copy-start(f32[48,512]{1,0:T(8,128)} %param.16) | copy-start | bytes 294916
  25.1 5.3 %copy-start.8 = (f32[48]{0:T(128)S(1)}, f32[48]{0:T(128)}, u32[]{:S(2)}) copy-start(f32[48]{0:T(128)} %param.15) | copy-start | bytes 580
  25.1 5.3 %copy-start.10 = (f32[8]{0:T(128)S(1)}, f32[8]{0:T(128)}, u32[]{:S(2)}) copy-start(f32[8]{0:T(128)} %param.14) | copy-start | bytes 100
  31.2 7.6 %collective-permute-start.3 = (f32[1,8,64]{2,1,0:T(8,128)S(1)}, f32[1,8,64]{2,1,0:T(8,128)S(1)}, u32[]{:S(2)}, u32[]{:S(2)}) collective-permute-start(f32[1,8,64]{2,1,0:T(8,128)S(1)} %slice.166), channel_id=1, source_target_pairs={{8,0},{16,8},{24,16},{32,24},{40,32},{48,40},{56,48},{64,56},{72,6... | collective-permute-start | bytes 6152 | tf_op jit(solution)/shard_map/ppermute | solution.py:19
  35.5 7.6 %collective-permute-start.2 = (f32[1,8,64]{2,1,0:T(8,128)S(1)}, f32[1,8,64]{2,1,0:T(8,128)S(1)}, u32[]{:S(2)}, u32[]{:S(2)}) collective-permute-start(f32[1,8,64]{2,1,0:T(8,128)S(1)} %slice.162), channel_id=1, source_target_pairs={{0,8},{8,16},{16,24},{24,32},{32,40},{40,48},{48,56},{56,64},{64,7... | collective-permute-start | bytes 6152 | tf_op jit(solution)/shard_map/ppermute | solution.py:16
  44.2 7.6 %collective-permute-start.5 = (f32[1,8,64]{2,1,0:T(8,128)S(1)}, f32[1,8,64]{2,1,0:T(8,128)S(1)}, u32[]{:S(2)}, u32[]{:S(2)}) collective-permute-start(f32[1,8,64]{2,1,0:T(8,128)S(1)} %slice.173), channel_id=1, source_target_pairs={{8,0},{16,8},{24,16},{32,24},{40,32},{48,40},{56,48},{64,56},{72,6... | collective-permute-start | bytes 6152 | tf_op jit(solution)/shard_map/ppermute | solution.py:19
  47.8 7.6 %collective-permute-start.4 = (f32[1,8,64]{2,1,0:T(8,128)S(1)}, f32[1,8,64]{2,1,0:T(8,128)S(1)}, u32[]{:S(2)}, u32[]{:S(2)}) collective-permute-start(f32[1,8,64]{2,1,0:T(8,128)S(1)} %slice.169), channel_id=1, source_target_pairs={{0,8},{8,16},{16,24},{24,32},{32,40},{40,48},{48,56},{56,64},{64,7... | collective-permute-start | bytes 6152 | tf_op jit(solution)/shard_map/ppermute | solution.py:16
  56.3 7.6 %collective-permute-start.7 = (f32[1,8,64]{2,1,0:T(8,128)S(1)}, f32[1,8,64]{2,1,0:T(8,128)S(1)}, u32[]{:S(2)}, u32[]{:S(2)}) collective-permute-start(f32[1,8,64]{2,1,0:T(8,128)S(1)} %slice.180), channel_id=1, source_target_pairs={{8,0},{16,8},{24,16},{32,24},{40,32},{48,40},{56,48},{64,56},{72,6... | collective-permute-start | bytes 6152 | tf_op jit(solution)/shard_map/ppermute | solution.py:19
  59.7 8.0 %copy-start.2 = (bf16[48,8,512]{2,1,0:T(8,128)(2,1)S(1)}, bf16[48,8,512]{2,1,0:T(8,128)(2,1)}, u32[]{:S(2)}) copy-start(bf16[48,8,512]{2,1,0:T(8,128)(2,1)} %param.12) | copy-start | bytes 1179652
  60.0 7.6 %collective-permute-start.6 = (f32[1,8,64]{2,1,0:T(8,128)S(1)}, f32[1,8,64]{2,1,0:T(8,128)S(1)}, u32[]{:S(2)}, u32[]{:S(2)}) collective-permute-start(f32[1,8,64]{2,1,0:T(8,128)S(1)} %slice.176), channel_id=1, source_target_pairs={{0,8},{8,16},{16,24},{24,32},{32,40},{40,48},{48,56},{56,64},{64,7... | collective-permute-start | bytes 6152 | tf_op jit(solution)/shard_map/ppermute | solution.py:16
  67.6 66.7 %copy-start.4 = (bf16[512,64]{0,1:T(8,128)(2,1)S(1)}, bf16[512,64]{0,1:T(8,128)(2,1)}, u32[]{:S(2)}) copy-start(bf16[512,64]{0,1:T(8,128)(2,1)} %param.19) | copy-start | bytes 196612
  67.7 99.5 %copy-start.6 = (f32[64,64]{1,0:T(8,128)S(1)}, f32[64,64]{1,0:T(8,128)}, u32[]{:S(2)}) copy-start(f32[64,64]{1,0:T(8,128)} %param.23) | copy-start | bytes 49156
  67.7 230.6 %copy-start.5 = (bf16[64,512]{1,0:T(8,128)(2,1)S(1)}, bf16[64,512]{1,0:T(8,128)(2,1)}, u32[]{:S(2)}) copy-start(bf16[64,512]{1,0:T(8,128)(2,1)} %param.20) | copy-start | bytes 196612
  70.5 65.9 %all-to-all-start = ((s32[64,1,2]{2,1,0:T(1,128)}), s32[64,1,2]{2,1,0:T(1,128)S(1)}, u32[]{:S(2)}, u32[]{:S(2)}) async-start(s32[64,1,2]{2,1,0:T(1,128)} %bitcast.2), calls=%async_computation | async-start | bytes 65536 | tf_op jit(solution)/shard_map/all_to_all | solution.py:103
  136.5 29.4 %all-to-all-start.1 = ((f32[64,1,128]{2,1,0:T(1,128)}), f32[64,1,128]{2,1,0:T(1,128)S(1)}, u32[]{:S(2)}, u32[]{:S(2)}) async-start(f32[64,1,128]{2,1,0:T(1,128)} %reshape.85), calls=%async_computation.1 | async-start | bytes 65536 | tf_op jit(solution)/shard_map/all_to_all | solution.py:102
  152.4 143.7 %all-gather.2.cloned.1.call-start = ((), (), s32[]{:S(2)}) async-start(), calls=%async_computation.3 | async-start | bytes 2129920 | tf_op jit(solution)/shard_map/all_gather | solution.py:112
  298.9 8.4 %collective-permute-start.9 = (f32[1,8,64]{2,1,0:T(8,128)S(1)}, f32[1,8,64]{2,1,0:T(8,128)S(1)}, u32[]{:S(2)}, u32[]{:S(2)}) collective-permute-start(f32[1,8,64]{2,1,0:T(8,128)S(1)} %slice.187), channel_id=1, source_target_pairs={{8,0},{16,8},{24,16},{32,24},{40,32},{48,40},{56,48},{64,56},{72,6... | collective-permute-start | bytes 6152 | tf_op jit(solution)/shard_map/ppermute | solution.py:19
  305.4 7.6 %collective-permute-start.8 = (f32[1,8,64]{2,1,0:T(8,128)S(1)}, f32[1,8,64]{2,1,0:T(8,128)S(1)}, u32[]{:S(2)}, u32[]{:S(2)}) collective-permute-start(f32[1,8,64]{2,1,0:T(8,128)S(1)} %slice.183), channel_id=1, source_target_pairs={{0,8},{8,16},{16,24},{24,32},{32,40},{40,48},{48,56},{56,64},{64,7... | collective-permute-start | bytes 6152 | tf_op jit(solution)/shard_map/ppermute | solution.py:16
Sparse Core Ops, SparseCore 0:
  69.9 64.3 all-reduce.1
  168.1 127.9 all-gather.1
where the time goes:
time: 321 us
  waiting for transfers between devices  213 us (66%)
  starting transfers between devices  59.2 us (18%)
  matrix products  20.7 us (6%)
  between operations  14.7 us (5%)
  local copies, waits for them, and re-layouts  7.21 us (2%)
  other arithmetic  5.72 us (2%)
    all_gather x1, waiting for transfers between devices, local(): every_pot = lax.all_gather(updated, 'dom', axis=0, tiled=True)  128 us
    psum x1, waiting for transfers between devices, local(): density_term = lax.psum(partial_density, 'orb')  58.1 us
    ppermute x5, starting transfers between devices, padded_2(): lax.ppermute(lax.slice_in_dim(block, 0, width, axis=dim), axis, backward)  22.6 us
    all_to_all x1, starting transfers between devices, local(): lax.all_to_all(send_values, 'dom', split_axis=0, concat_axis=0, tiled=True)  15.9 us
    ppermute x5, waiting for transfers between devices, padded_2(): lax.ppermute(lax.slice_in_dim(block, block.shape[dim] - width, None, axis...  15 us
    ppermute x5, starting transfers between devices, padded_2(): lax.ppermute(lax.slice_in_dim(block, block.shape[dim] - width, None, axis...  15 us
    all_to_all x1, waiting for transfers between devices, local(): lax.all_to_all(send_values, 'dom', split_axis=0, concat_axis=0, tiled=True)  12 us
    dot_general x5, matrix products, assemble_local(): jnp.einsum('ckj,coj->cok', onehot, left_next, precision=lax.Precision.HIG...  7.2 us
  transfers between devices with their start and end apart: 14, of which 8 were waited for; matrix products, arithmetic and copies ran while one was open for 6% of the time, Pallas kernels for 0%

commit v1 on v0

--- a/solution.py
+++ b/solution.py
@@ -109,7 +109,10 @@
         recv_hot, recv_values.reshape(-1, coarse_cols), precision=lax.Precision.HIGHEST
     )
     updated = potential - step_rate * summed
-    every_pot = lax.all_gather(updated, "dom", axis=0, tiled=True)
+    size = lax.axis_size("dom")
+    blocks = jnp.stack([updated for _ in range(size)])
+    blocks = lax.all_to_all(blocks, "dom", split_axis=0, concat_axis=0)
+    every_pot = jnp.concatenate(blocks, axis=0)
     cell_pot = every_pot[dest_owner * pot_rows + pot_slot]
     node_potential = jnp.dot(cell_pot, prolong.astype(jnp.float32), precision=lax.Precision.HIGHEST)
     shift_new = (base_potential + node_potential)[:, None, :]

time: 321 us -> 253 us (0.79)
  the two profiles are of different devices: /device:TPU:2 before, /device:TPU:30 now
where the time goes in v1:
time: 253 us
  waiting for transfers between devices  132 us (52%)
  starting transfers between devices  65.2 us (26%)
  matrix products  20.1 us (8%)
  between operations  14.7 us (6%)
  local copies, waits for them, and re-layouts  11.9 us (5%)
  other arithmetic  8.99 us (4%)
    psum x1, waiting for transfers between devices, local(): density_term = lax.psum(partial_density, 'orb')  55.3 us
    all_to_all x1, waiting for transfers between devices, local(): blocks = lax.all_to_all(blocks, 'dom', split_axis=0, concat_axis=0)  52.5 us
    ppermute x5, starting transfers between devices, padded_2(): lax.ppermute(lax.slice_in_dim(block, 0, width, axis=dim), axis, backward)  20 us
    ppermute x5, starting transfers between devices, padded_2(): lax.ppermute(lax.slice_in_dim(block, block.shape[dim] - width, None, axis...  17 us
    all_to_all x1, starting transfers between devices, local(): lax.all_to_all(send_values, 'dom', split_axis=0, concat_axis=0, tiled=True)  16.1 us
    ppermute x5, waiting for transfers between devices, padded_2(): lax.ppermute(lax.slice_in_dim(block, block.shape[dim] - width, None, axis...  13 us
    all_to_all x1, waiting for transfers between devices, local(): lax.all_to_all(send_values, 'dom', split_axis=0, concat_axis=0, tiled=True)  11.1 us
    dot_general x5, matrix products, assemble_local(): jnp.einsum('ckj,coj->cok', onehot, left_next, precision=lax.Precision.HIG...  7.2 us
  transfers between devices with their start and end apart: 14, of which 8 were waited for; matrix products, arithmetic and copies ran while one was open for 8% of the time, Pallas kernels for 0%

profile of v1, /device:TPU:30, one launch (start us, length us, event | category | flops | bytes accessed | tf_op | source)
XLA Modules:
  0.0 252.7 jit_solution(2680980851029094778)
XLA Ops:
  7.3 1.0 copy-done
  8.2 1.6 fusion.10
  9.8 11.7 %collective-permute-start.1 = (f32[1,8,64]{2,1,0:T(8,128)S(1)}, f32[1,8,64]{2,1,0:T(8,128)S(1)}, u32[]{:S(2)}, u32[]{:S(2)}) collective-permute-start(f32[1,8,64]{2,1,0:T(8,128)S(1)} %slice.159), channel_id=1, source_target_pairs={{8,0},{16,8},{24,16},{32,24},{40,32},{48,40},{56,48},{64,56},{72,6... | collective-permute-start | bytes 6152 | tf_op jit(solution)/shard_map/ppermute | solution.py:19
  21.5 1.4 fusion.9
  22.9 1.9 collective-permute-start
  25.7 1.4 fusion.15
  27.1 3.5 %collective-permute-done = f32[1,8,64]{2,1,0:T(8,128)S(1)} collective-permute-done((f32[1,8,64]{2,1,0:T(8,128)S(1)}, f32[1,8,64]{2,1,0:T(8,128)S(1)}, u32[]{:S(2)}, u32[]{:S(2)}) %collective-permute-start) | collective-permute-done | bytes 2080 | tf_op jit(solution)/shard_map/ppermute | solution.py:16
  30.6 0.8 fusion.11
  31.5 2.6 %collective-permute-start.3 = (f32[1,8,64]{2,1,0:T(8,128)S(1)}, f32[1,8,64]{2,1,0:T(8,128)S(1)}, u32[]{:S(2)}, u32[]{:S(2)}) collective-permute-start(f32[1,8,64]{2,1,0:T(8,128)S(1)} %slice.166), channel_id=1, source_target_pairs={{8,0},{16,8},{24,16},{32,24},{40,32},{48,40},{56,48},{64,56},{72,6... | collective-permute-start | bytes 6152 | tf_op jit(solution)/shard_map/ppermute | solution.py:19
  34.1 1.4 fusion.7
  35.8 3.3 %collective-permute-start.2 = (f32[1,8,64]{2,1,0:T(8,128)S(1)}, f32[1,8,64]{2,1,0:T(8,128)S(1)}, u32[]{:S(2)}, u32[]{:S(2)}) collective-permute-start(f32[1,8,64]{2,1,0:T(8,128)S(1)} %slice.162), channel_id=1, source_target_pairs={{0,8},{8,16},{16,24},{24,32},{32,40},{40,48},{48,56},{56,64},{64,7... | collective-permute-start | bytes 6152 | tf_op jit(solution)/shard_map/ppermute | solution.py:16
  39.1 1.4 fusion.16
  40.5 2.9 %collective-permute-done.2 = f32[1,8,64]{2,1,0:T(8,128)S(1)} collective-permute-done((f32[1,8,64]{2,1,0:T(8,128)S(1)}, f32[1,8,64]{2,1,0:T(8,128)S(1)}, u32[]{:S(2)}, u32[]{:S(2)}) %collective-permute-start.2) | collective-permute-done | bytes 2080 | tf_op jit(solution)/shard_map/ppermute | solution.py:16
  43.5 0.6 fusion.27
  44.5 1.9 collective-permute-start.5
  46.4 1.4 fusion.5
  48.1 3.9 %collective-permute-start.4 = (f32[1,8,64]{2,1,0:T(8,128)S(1)}, f32[1,8,64]{2,1,0:T(8,128)S(1)}, u32[]{:S(2)}, u32[]{:S(2)}) collective-permute-start(f32[1,8,64]{2,1,0:T(8,128)S(1)} %slice.169), channel_id=1, source_target_pairs={{0,8},{8,16},{16,24},{24,32},{32,40},{40,48},{48,56},{56,64},{64,7... | collective-permute-start | bytes 6152 | tf_op jit(solution)/shard_map/ppermute | solution.py:16
  52.1 1.4 fusion.17
  53.5 2.3 collective-permute-done.4
  55.8 0.8 fusion.13
  56.6 1.9 collective-permute-start.7
  58.5 1.4 fusion.3
  60.3 3.9 %collective-permute-start.6 = (f32[1,8,64]{2,1,0:T(8,128)S(1)}, f32[1,8,64]{2,1,0:T(8,128)S(1)}, u32[]{:S(2)}, u32[]{:S(2)}) collective-permute-start(f32[1,8,64]{2,1,0:T(8,128)S(1)} %slice.176), channel_id=1, source_target_pairs={{0,8},{8,16},{16,24},{24,32},{32,40},{40,48},{48,56},{56,64},{64,7... | collective-permute-start | bytes 6152 | tf_op jit(solution)/shard_map/ppermute | solution.py:16
  64.2 1.4 fusion.18
  65.6 2.3 collective-permute-done.6
  68.0 2.1 fusion.24
  70.1 0.7 sub.46
  70.8 5.5 %all-to-all-start = ((s32[64,1,2]{2,1,0:T(1,128)}), s32[64,1,2]{2,1,0:T(1,128)S(1)}, u32[]{:S(2)}, u32[]{:S(2)}) async-start(s32[64,1,2]{2,1,0:T(1,128)} %bitcast.2), calls=%async_computation | async-start | bytes 65536 | tf_op jit(solution)/shard_map/all_to_all | solution.py:103
  76.4 55.3 %all-reduce.2.cloned.1.call-done = f32[48,512]{1,0:T(8,128)} async-done(((f32[48,512]{1,0:T(8,128)}), f32[48,512]{1,0:T(8,128)}) %all-reduce.2.cloned.1.call-update) | async-done | bytes 98320 | tf_op jit(solution)/shard_map/psum | solution.py:81
  131.7 1.1 fusion.90
  133.1 0.7 reshape.91
  133.8 16.1 %all-to-all-start.1 = ((f32[64,1,128]{2,1,0:T(1,128)}), f32[64,1,128]{2,1,0:T(1,128)S(1)}, u32[]{:S(2)}, u32[]{:S(2)}) async-start(f32[64,1,128]{2,1,0:T(1,128)} %reshape.91), calls=%async_computation.1 | async-start | bytes 65536 | tf_op jit(solution)/shard_map/all_to_all | solution.py:102
  149.9 0.5 broadcast.72
  150.5 0.7 reduce.3
  151.3 11.1 %all-to-all-done.1 = f32[64,1,128]{2,1,0:T(1,128)S(1)} async-done(((f32[64,1,128]{2,1,0:T(1,128)}), f32[64,1,128]{2,1,0:T(1,128)S(1)}, u32[]{:S(2)}, u32[]{:S(2)}) %all-to-all-start.1) | async-done | bytes 32800 | tf_op jit(solution)/shard_map/all_to_all | solution.py:102
  162.9 0.7 reduce.4
  164.2 2.3 reshape.93
  166.5 6.5 %all-to-all-start.2 = ((f32[64,1,4096]{2,1,0:T(1,128)}), f32[64,1,4096]{2,1,0:T(1,128)S(1)}, u32[]{:S(2)}, u32[]{:S(2)}) async-start(f32[64,1,4096]{2,1,0:T(1,128)} %reshape.93), calls=%async_computation.2 | async-start | bytes 2097152 | tf_op jit(solution)/shard_map/all_to_all | solution.py:114
  173.0 52.5 %all-to-all-done.2 = f32[64,1,4096]{2,1,0:T(1,128)S(1)} async-done(((f32[64,1,4096]{2,1,0:T(1,128)}), f32[64,1,4096]{2,1,0:T(1,128)S(1)}, u32[]{:S(2)}, u32[]{:S(2)}) %all-to-all-start.2) | async-done | bytes 1048608 | tf_op jit(solution)/shard_map/all_to_all | solution.py:114
  225.5 3.3 %reduce.5 = f32[64,4096]{1,0:T(8,128)S(1)} reduce(f32[64,1,4096]{2,1,0:T(1,128)S(1)} %all-to-all-done.2, f32[]{:T(128)} %broadcast.74), dimensions={1}, to_apply=%all_to_all.12.reduce_sub_computation | reduce | bytes 2097156 | tf_op jit(solution)/shard_map/all_to_all | solution.py:114
  228.8 2.2 reshape.94
  230.9 2.2 gather_fusion
  233.7 1.9 collective-permute-start.9
  235.6 1.4 fusion.1
  237.3 3.9 %collective-permute-start.8 = (f32[1,8,64]{2,1,0:T(8,128)S(1)}, f32[1,8,64]{2,1,0:T(8,128)S(1)}, u32[]{:S(2)}, u32[]{:S(2)}) collective-permute-start(f32[1,8,64]{2,1,0:T(8,128)S(1)} %slice.183), channel_id=1, source_target_pairs={{0,8},{8,16},{16,24},{24,32},{32,40},{40,48},{48,56},{56,64},{64,7... | collective-permute-start | bytes 6152 | tf_op jit(solution)/shard_map/ppermute | solution.py:16
  241.2 1.6 fusion.20
  242.8 2.1 collective-permute-done.8
  244.9 1.0 pad_maximum_fusion
  (79 shorter events, 4.5 us)
Async XLA Ops:
  7.2 1.0 copy-start
  7.2 14.3 %copy-start.12 = (s32[48,64]{1,0:T(8,128)S(1)}, s32[48,64]{1,0:T(8,128)}, u32[]{:S(2)}) copy-start(s32[48,64]{1,0:T(8,128)} %param.18) | copy-start | bytes 36868
  7.2 17.7 %copy-start.8 = (s32[48,1]{0,1:T(1,128)S(1)}, s32[48,1]{0,1:T(1,128)}, u32[]{:S(2)}) copy-start(s32[48,1]{0,1:T(1,128)} %param.21) | copy-start | bytes 580
  7.2 18.0 %copy-start.10 = (s32[48]{0:T(128)S(1)}, s32[48]{0:T(128)}, u32[]{:S(2)}) copy-start(s32[48]{0:T(128)} %param.22) | copy-start | bytes 580
  7.2 124.5 %all-reduce.2.cloned.1.call-start = ((), (), s32[]{:S(2)}) async-start(), calls=%async_computation.3 | async-start | bytes 196608 | tf_op jit(solution)/shard_map/psum | solution.py:81
  9.8 15.8 %collective-permute-start.1 = (f32[1,8,64]{2,1,0:T(8,128)S(1)}, f32[1,8,64]{2,1,0:T(8,128)S(1)}, u32[]{:S(2)}, u32[]{:S(2)}) collective-permute-start(f32[1,8,64]{2,1,0:T(8,128)S(1)} %slice.159), channel_id=1, source_target_pairs={{8,0},{16,8},{24,16},{32,24},{40,32},{48,40},{56,48},{64,56},{72,6... | collective-permute-start | bytes 6152 | tf_op jit(solution)/shard_map/ppermute | solution.py:19
  22.9 7.6 %collective-permute-start = (f32[1,8,64]{2,1,0:T(8,128)S(1)}, f32[1,8,64]{2,1,0:T(8,128)S(1)}, u32[]{:S(2)}, u32[]{:S(2)}) collective-permute-start(f32[1,8,64]{2,1,0:T(8,128)S(1)} %slice.155), channel_id=1, source_target_pairs={{0,8},{8,16},{16,24},{24,32},{32,40},{40,48},{48,56},{56,64},{64,7... | collective-permute-start | bytes 6152 | tf_op jit(solution)/shard_map/ppermute | solution.py:16
  25.3 5.3 %copy-start.1 = (bf16[48,8,512]{2,1,0:T(8,128)(2,1)S(1)}, bf16[48,8,512]{2,1,0:T(8,128)(2,1)}, u32[]{:S(2)}) copy-start(bf16[48,8,512]{2,1,0:T(8,128)(2,1)} %param.13) | copy-start | bytes 1179652
  25.3 5.3 %copy-start.3 = (f32[48,512]{1,0:T(8,128)S(1)}, f32[48,512]{1,0:T(8,128)}, u32[]{:S(2)}) copy-start(f32[48,512]{1,0:T(8,128)} %param.16) | copy-start | bytes 294916
  25.4 5.3 %copy-start.9 = (f32[48]{0:T(128)S(1)}, f32[48]{0:T(128)}, u32[]{:S(2)}) copy-start(f32[48]{0:T(128)} %param.15) | copy-start | bytes 580
  25.4 5.3 %copy-start.11 = (f32[8]{0:T(128)S(1)}, f32[8]{0:T(128)}, u32[]{:S(2)}) copy-start(f32[8]{0:T(128)} %param.14) | copy-start | bytes 100
  31.5 7.6 %collective-permute-start.3 = (f32[1,8,64]{2,1,0:T(8,128)S(1)}, f32[1,8,64]{2,1,0:T(8,128)S(1)}, u32[]{:S(2)}, u32[]{:S(2)}) collective-permute-start(f32[1,8,64]{2,1,0:T(8,128)S(1)} %slice.166), channel_id=1, source_target_pairs={{8,0},{16,8},{24,16},{32,24},{40,32},{48,40},{56,48},{64,56},{72,6... | collective-permute-start | bytes 6152 | tf_op jit(solution)/shard_map/ppermute | solution.py:19
  35.8 7.6 %collective-permute-start.2 = (f32[1,8,64]{2,1,0:T(8,128)S(1)}, f32[1,8,64]{2,1,0:T(8,128)S(1)}, u32[]{:S(2)}, u32[]{:S(2)}) collective-permute-start(f32[1,8,64]{2,1,0:T(8,128)S(1)} %slice.162), channel_id=1, source_target_pairs={{0,8},{8,16},{16,24},{24,32},{32,40},{40,48},{48,56},{56,64},{64,7... | collective-permute-start | bytes 6152 | tf_op jit(solution)/shard_map/ppermute | solution.py:16
  44.5 7.6 %collective-permute-start.5 = (f32[1,8,64]{2,1,0:T(8,128)S(1)}, f32[1,8,64]{2,1,0:T(8,128)S(1)}, u32[]{:S(2)}, u32[]{:S(2)}) collective-permute-start(f32[1,8,64]{2,1,0:T(8,128)S(1)} %slice.173), channel_id=1, source_target_pairs={{8,0},{16,8},{24,16},{32,24},{40,32},{48,40},{56,48},{64,56},{72,6... | collective-permute-start | bytes 6152 | tf_op jit(solution)/shard_map/ppermute | solution.py:19
  48.1 7.6 %collective-permute-start.4 = (f32[1,8,64]{2,1,0:T(8,128)S(1)}, f32[1,8,64]{2,1,0:T(8,128)S(1)}, u32[]{:S(2)}, u32[]{:S(2)}) collective-permute-start(f32[1,8,64]{2,1,0:T(8,128)S(1)} %slice.169), channel_id=1, source_target_pairs={{0,8},{8,16},{16,24},{24,32},{32,40},{40,48},{48,56},{56,64},{64,7... | collective-permute-start | bytes 6152 | tf_op jit(solution)/shard_map/ppermute | solution.py:16
  56.6 7.6 %collective-permute-start.7 = (f32[1,8,64]{2,1,0:T(8,128)S(1)}, f32[1,8,64]{2,1,0:T(8,128)S(1)}, u32[]{:S(2)}, u32[]{:S(2)}) collective-permute-start(f32[1,8,64]{2,1,0:T(8,128)S(1)} %slice.180), channel_id=1, source_target_pairs={{8,0},{16,8},{24,16},{32,24},{40,32},{48,40},{56,48},{64,56},{72,6... | collective-permute-start | bytes 6152 | tf_op jit(solution)/shard_map/ppermute | solution.py:19
  60.0 8.0 %copy-start.2 = (bf16[48,8,512]{2,1,0:T(8,128)(2,1)S(1)}, bf16[48,8,512]{2,1,0:T(8,128)(2,1)}, u32[]{:S(2)}) copy-start(bf16[48,8,512]{2,1,0:T(8,128)(2,1)} %param.12) | copy-start | bytes 1179652
  60.3 7.6 %collective-permute-start.6 = (f32[1,8,64]{2,1,0:T(8,128)S(1)}, f32[1,8,64]{2,1,0:T(8,128)S(1)}, u32[]{:S(2)}, u32[]{:S(2)}) collective-permute-start(f32[1,8,64]{2,1,0:T(8,128)S(1)} %slice.176), channel_id=1, source_target_pairs={{0,8},{8,16},{16,24},{24,32},{32,40},{40,48},{48,56},{56,64},{64,7... | collective-permute-start | bytes 6152 | tf_op jit(solution)/shard_map/ppermute | solution.py:16
  67.9 63.8 %copy-start.5 = (bf16[512,64]{0,1:T(8,128)(2,1)S(1)}, bf16[512,64]{0,1:T(8,128)(2,1)}, u32[]{:S(2)}) copy-start(bf16[512,64]{0,1:T(8,128)(2,1)} %param.19) | copy-start | bytes 196612
  67.9 95.8 %copy-start.7 = (f32[64,64]{1,0:T(8,128)S(1)}, f32[64,64]{1,0:T(8,128)}, u32[]{:S(2)}) copy-start(f32[64,64]{1,0:T(8,128)} %param.23) | copy-start | bytes 49156
  70.8 63.0 %all-to-all-start = ((s32[64,1,2]{2,1,0:T(1,128)}), s32[64,1,2]{2,1,0:T(1,128)S(1)}, u32[]{:S(2)}, u32[]{:S(2)}) async-start(s32[64,1,2]{2,1,0:T(1,128)} %bitcast.2), calls=%async_computation | async-start | bytes 65536 | tf_op jit(solution)/shard_map/all_to_all | solution.py:103
  133.8 28.6 %all-to-all-start.1 = ((f32[64,1,128]{2,1,0:T(1,128)}), f32[64,1,128]{2,1,0:T(1,128)S(1)}, u32[]{:S(2)}, u32[]{:S(2)}) async-start(f32[64,1,128]{2,1,0:T(1,128)} %reshape.91), calls=%async_computation.1 | async-start | bytes 65536 | tf_op jit(solution)/shard_map/all_to_all | solution.py:102
  163.9 2.5 %copy-start.4 = (f32[64,64]{1,0:T(8,128)}, f32[64,64]{1,0:T(8,128)S(1)}, u32[]{:S(2)}) copy-start(f32[64,64]{1,0:T(8,128)S(1)} %fusion.21) | copy-start | bytes 49156
  166.5 59.0 %all-to-all-start.2 = ((f32[64,1,4096]{2,1,0:T(1,128)}), f32[64,1,4096]{2,1,0:T(1,128)S(1)}, u32[]{:S(2)}, u32[]{:S(2)}) async-start(f32[64,1,4096]{2,1,0:T(1,128)} %reshape.93), calls=%async_computation.2 | async-start | bytes 2097152 | tf_op jit(solution)/shard_map/all_to_all | solution.py:114
  228.8 4.4 %copy-start.6 = (bf16[64,512]{1,0:T(8,128)(2,1)S(1)}, bf16[64,512]{1,0:T(8,128)(2,1)}, u32[]{:S(2)}) copy-start(bf16[64,512]{1,0:T(8,128)(2,1)} %param.20) | copy-start | bytes 196612
  233.7 7.5 %collective-permute-start.9 = (f32[1,8,64]{2,1,0:T(8,128)S(1)}, f32[1,8,64]{2,1,0:T(8,128)S(1)}, u32[]{:S(2)}, u32[]{:S(2)}) collective-permute-start(f32[1,8,64]{2,1,0:T(8,128)S(1)} %slice.187), channel_id=1, source_target_pairs={{8,0},{16,8},{24,16},{32,24},{40,32},{48,40},{56,48},{64,56},{72,6... | collective-permute-start | bytes 6152 | tf_op jit(solution)/shard_map/ppermute | solution.py:19
  237.3 7.6 %collective-permute-start.8 = (f32[1,8,64]{2,1,0:T(8,128)S(1)}, f32[1,8,64]{2,1,0:T(8,128)S(1)}, u32[]{:S(2)}, u32[]{:S(2)}) collective-permute-start(f32[1,8,64]{2,1,0:T(8,128)S(1)} %slice.183), channel_id=1, source_target_pairs={{0,8},{8,16},{16,24},{24,32},{32,40},{40,48},{48,56},{56,64},{64,7... | collective-permute-start | bytes 6152 | tf_op jit(solution)/shard_map/ppermute | solution.py:16
Sparse Core Ops, SparseCore 0:
  70.2 61.4 all-reduce.1
